TPU v7x, 32 devices: a whole 2x2x4 slice. The times are simulated.
32 devices in a mesh: row: 8 (over z, y), col: 4 (over x, core).
Axes of the slice: x: 2, y: 2, z: 4, core: 2. Of those that a mesh axis runs over, the one named last changes fastest.
Arguments:
- couple_features: bfloat16 [256, 256, 128], P('row', 'col'), may hold values from -6 to 6
- homolog_features: bfloat16 [48, 256, 64], P('col', 'row'), may hold values from -6 to 6
- genuine_position_flags: int32 [256], P('row'), may hold values from 0 to 1, as said below
- homolog_availability: int32 [48], P('col'), may hold values from 0 to 1, as said below
- primary_factor_matrix: bfloat16 [64, 32], replicated, may hold values from -0.75 to 0.75
- secondary_factor_matrix: bfloat16 [64, 32], replicated, may hold values from -0.75 to 0.75
- contraction_matrix: bfloat16 [1024, 128], replicated, may hold values from -0.1875 to 0.1875
- contraction_offset: float32 [128], replicated, may hold values from -3 to 3
- attention_score_matrix: bfloat16 [128, 8], replicated, may hold values from -100 to 100
- content_projection_matrix: bfloat16 [64, 256], replicated, may hold values from -0.75 to 0.75
- sigmoid_switch_matrix: bfloat16 [64, 256], replicated, may hold values from -0.75 to 0.75
- final_projection_matrix: bfloat16 [256, 64], replicated, may hold values from -0.375 to 0.375
Outputs:
- pair_output: bfloat16 [256, 256, 128], P('row', 'col')
- refreshed_homologs: bfloat16 [48, 256, 64], P('col', 'row')
Inputs may be any that keep to these rules, and one draw needn't show every extreme that they name: `genuine_position_flags`: entry 0 is 1 and the last entry is 0. `homolog_availability`: entry 0 is 1 and the last entry is 0.
All inputs are finite; a program needn't handle non-finite values.
Results may differ from a plain program's by a relative error of at most 0.0093.
Values may be sent and summed in bfloat16 or wider, within the bound.
A program may use at most 64 MiB of HBM per device.

v0:
```python
import math

import jax
import jax.numpy as jnp
from jax import lax
from jax.sharding import PartitionSpec as P

EPSILON = 1e-05


def standardize_features(inputs):
    mean_value = jnp.mean(inputs, axis=-1, keepdims=True)
    centered = inputs - mean_value
    variance = jnp.mean(centered * centered, axis=-1, keepdims=True)
    return centered * lax.rsqrt(variance + EPSILON)


def body(
    couple_features,
    homolog_features,
    genuine_position_flags,
    homolog_availability,
    primary_factor_matrix,
    secondary_factor_matrix,
    contraction_matrix,
    contraction_offset,
    attention_score_matrix,
    content_projection_matrix,
    sigmoid_switch_matrix,
    final_projection_matrix,
):
    local_homolog_flags = homolog_features.shape[0]
    homolog_flags = homolog_features.shape[1]
    position_flags = couple_features.shape[1]
    opm_width = primary_factor_matrix.shape[1]
    head_count = attention_score_matrix.shape[1]
    head_width = content_projection_matrix.shape[1] // head_count
    col_index = lax.axis_index("col")
    seq_marks = homolog_availability.astype(jnp.bfloat16).reshape(local_homolog_flags, 1, 1)
    tok_marks = genuine_position_flags.astype(jnp.bfloat16).reshape(1, homolog_flags, 1)
    alignment_rows, sequence_everything = (
        lax.all_gather(homolog_features, "col", axis=0, tiled=True),
        lax.all_gather(seq_marks, "col", axis=0, tiled=True),
    )
    sequence_overall = alignment_rows.shape[0]
    expanded_homologs, broad_token = (
        lax.all_gather(homolog_features, "row", axis=1, tiled=True),
        lax.all_gather(tok_marks, "row", axis=1, tiled=True),
    )
    position_offset = col_index * position_flags
    tok_cols = lax.dynamic_slice_in_dim(broad_token, position_offset, position_flags, 1)
    local_positions = lax.all_to_all(
        expanded_homologs, "col", split_axis=1, concat_axis=0, tiled=True
    )
    sequence_mask_float = sequence_everything.astype(jnp.float32)
    normed_rows = standardize_features(alignment_rows.astype(jnp.float32)).astype(jnp.bfloat16)
    normed_columns = standardize_features(local_positions.astype(jnp.float32)).astype(jnp.bfloat16)
    left_projected = (
        jnp.dot(normed_rows, primary_factor_matrix, preferred_element_type=jnp.float32)
        * sequence_mask_float
    ).astype(jnp.bfloat16)
    right_projected = (
        jnp.dot(normed_columns, secondary_factor_matrix, preferred_element_type=jnp.float32)
        * sequence_mask_float
    ).astype(jnp.bfloat16)
    seq_count = jnp.sum(sequence_mask_float)
    block_rows = math.gcd(homolog_flags, 16)
    blocks = homolog_flags // block_rows
    left_blocks = left_projected.reshape(sequence_overall, blocks, block_rows, opm_width).transpose(
        1, 0, 2, 3
    )

    def outer_block(left_block):
        outer = jnp.einsum(
            "sic,sjd->ijcd", left_block, right_projected, preferred_element_type=jnp.float32
        )
        outer = outer.astype(jnp.bfloat16).reshape(
            block_rows * position_flags, opm_width * opm_width
        )
        return jnp.dot(outer, contraction_matrix, preferred_element_type=jnp.float32).reshape(
            block_rows, position_flags, -1
        )

    update = (
        lax.map(outer_block, left_blocks).reshape(homolog_flags, position_flags, -1) / seq_count
        + contraction_offset
    )
    tok_row_f = genuine_position_flags.astype(jnp.float32)
    tok_col_f = tok_cols.reshape(position_flags).astype(jnp.float32)
    pair_output = (
        couple_features.astype(jnp.float32)
        + tok_row_f[:, None, None] * tok_col_f[None, :, None] * update
    ).astype(jnp.bfloat16)
    pair_norm = standardize_features(pair_output.astype(jnp.float32)).astype(jnp.bfloat16)
    logits = (
        jnp.dot(pair_norm, attention_score_matrix, preferred_element_type=jnp.float32)
        + ((tok_col_f - 1.0) * 1000000000.0)[None, :, None]
    )
    row_top = lax.pmax(jnp.max(logits, axis=1), "col")
    expd = jnp.exp(logits - row_top[:, None, :])
    row_total = lax.psum(jnp.sum(expd, axis=1), "col")
    weights = (expd / row_total[:, None, :]).astype(jnp.bfloat16)
    value_rows_gathered = jnp.dot(
        normed_columns, content_projection_matrix, preferred_element_type=jnp.float32
    ).astype(jnp.bfloat16)
    values_heads = value_rows_gathered.reshape(
        sequence_overall, position_flags, head_count, head_width
    )
    summed = jnp.einsum("ijh,sjhc->sihc", weights, values_heads, preferred_element_type=jnp.float32)
    full_sums = lax.psum(
        summed.reshape(sequence_overall, homolog_flags, head_count * head_width), "col"
    )
    own_sums = lax.dynamic_slice_in_dim(
        full_sums, col_index * local_homolog_flags, local_homolog_flags, 0
    )
    norm_own = lax.dynamic_slice_in_dim(
        normed_rows, col_index * local_homolog_flags, local_homolog_flags, 0
    )
    gate_values = jax.nn.sigmoid(
        jnp.dot(norm_own, sigmoid_switch_matrix, preferred_element_type=jnp.float32)
    )
    switched_result = (gate_values * own_sums).astype(jnp.bfloat16)
    refreshed_homologs = (
        homolog_features.astype(jnp.float32)
        + jnp.dot(switched_result, final_projection_matrix, preferred_element_type=jnp.float32)
    ).astype(jnp.bfloat16)
    return (pair_output, refreshed_homologs)


def solution(mesh):
    placed = (
        P("row", "col", None),
        P("col", "row", None),
        P("row"),
        P("col"),
        P(),
        P(),
        P(),
        P(),
        P(),
        P(),
        P(),
        P(),
    )
    return jax.shard_map(
        body,
        mesh=mesh,
        in_specs=placed,
        out_specs=(P("row", "col", None), P("col", "row", None)),
        check_vma=False,
    )
```

profile of v0, /device:TPU:13, one launch (start us, length us, event | category | flops | bytes accessed | tf_op | source)
XLA Modules:
  0.0 195.1 jit_solution(16748989459347077178)
XLA Ops:
  7.2 24.8 %all_gather.15 = bf16[12,256,64]{2,1,0:T(8,128)(2,1)S(1)} all-gather(bf16[12,32,64]{2,1,0:T(8,128)(2,1)} %param.15), channel_id=1, replica_groups=mesh['row'=8,'col'=4] {'row'}, dimensions={1}, use_global_device_ids=true | all-gather | bytes 442368 | tf_op jit(solution)/shard_map/all_gather | solution.py:47
  32.0 0.5 copy.117
  32.6 1.3 reshape.169
  33.9 10.1 %all-to-all-start = ((bf16[4,2,24576]{2,1,0:T(2,128)(2,1)}), bf16[4,2,24576]{2,1,0:T(2,128)(2,1)S(1)}, u32[]{:S(2)}, u32[]{:S(2)}) async-start(bf16[4,2,24576]{2,1,0:T(2,128)(2,1)} %reshape.169), calls=%async_computation | async-start | bytes 786432 | tf_op jit(solution)/shard_map/all_to_all | solution.py:52
  44.0 10.2 %all_gather.13 = bf16[48,32,64]{2,1,0:T(8,128)(2,1)S(1)} all-gather(bf16[12,32,64]{2,1,0:T(8,128)(2,1)S(1)} %copy-done.6), channel_id=1, replica_groups=mesh['row'=8,'col'=4] {'col'}, dimensions={0}, use_global_device_ids=true | all-gather | bytes 245760 | tf_op jit(solution)/shard_map/all_gather | solution.py:42
  54.2 0.6 dynamic-slice.2
  55.5 0.2 dynamic-update-slice.1
  55.7 5.2 %all-reduce.1 = bf16[48]{0:T(256)(128)(2,1)S(1)} all-reduce(bf16[48]{0:T(256)(128)(2,1)S(1)} %dynamic-update-slice.1), channel_id=3, replica_groups=mesh['row'=8,'col'=4] {'col'}, use_global_device_ids=true, to_apply=%add.1 | all-reduce | flops 48 | bytes 192
  60.9 0.3 convert_reduce_fusion.1
  61.2 0.5 fusion.26
  61.7 0.5 fusion.27
  62.2 0.6 dynamic-slice.1
  63.5 0.2 dynamic-update-slice
  63.7 13.1 %all-reduce = bf16[256]{0:T(256)(128)(2,1)S(1)} all-reduce(bf16[256]{0:T(256)(128)(2,1)S(1)} %dynamic-update-slice), channel_id=2, replica_groups=mesh['row'=8,'col'=4] {'row'}, use_global_device_ids=true, to_apply=%add | all-reduce | flops 256 | bytes 1024
  76.8 0.7 add_multiply_fusion
  77.6 0.6 convert_reduce_fusion.2
  78.2 0.6 fusion.15
  78.8 0.6 reshape.170
  79.4 0.7 copy.92
  80.1 0.7 reshape.136
  81.0 0.5 multiply_reduce_fusion
  81.6 0.6 rsqrt.29
  82.2 0.6 div.43
  82.8 0.7 copy.93
  83.5 1.7 fusion.7
  85.3 0.8 fusion.8
  86.3 0.3 copy-done.4
  86.6 8.6 %while.10 = (s32[]{:T(128)}, f32[2,16,64,128]{3,2,1,0:T(8,128)S(1)}, bf16[2,48,16,32]{1,3,2,0:T(8,128)(2,1)S(1)}, bf16[48,64,32]{1,0,2:T(8,128)(2,1)S(1)}, bf16[1024,128]{1,0:T(8,128)(2,1)S(1)}, /*index=5*/s32[]{:T(128)}) while((s32[]{:T(128)}, f32[2,16,64,128]{3,2,1,0:T(8,128)S(1)}, bf16[2,48,16,32]{1,3,2,0:T(8,128)(2,1)S(1)}, ...), condition=%wide.region_5.6_spmd, body=%wide.region_4.0_spmd.sunk | while | flops 370147328 | bytes 11796557 | solution.py:85
  86.6 1.2 convert_bitcast_fusion.2
  87.8 1.8 copy.119
  89.6 1.3 fusion.65
  90.9 1.2 convert_bitcast_fusion.2
  92.1 1.8 copy.119
  93.9 1.3 fusion.65
  95.2 0.7 broadcast_divide_fusion
  95.9 0.3 copy-done.5
  96.2 0.3 fusion.23
  96.6 0.3 convert_reduce_fusion
  96.9 0.6 fusion.20
  97.6 0.8 fusion.51
  98.4 13.8 %pmax.7 = f32[32,8]{1,0:T(8,128)S(1)} all-reduce(f32[32,8]{1,0:T(8,128)S(1)} %get-tuple-element.79), channel_id=1, replica_groups=mesh['row'=8,'col'=4] {'col'}, use_global_device_ids=true, to_apply=%region_10.11 | all-reduce | flops 256 | bytes 2048 | tf_op jit(solution)/shard_map/pmax | solution.py:99
  112.4 10.3 %psum.14 = f32[32,8]{1,0:T(8,128)S(1)} all-reduce(f32[32,8]{1,0:T(8,128)S(1)} %fusion.34), channel_id=1, replica_groups=mesh['row'=8,'col'=4] {'col'}, use_global_device_ids=true, to_apply=%region_12.13 | all-reduce | flops 256 | bytes 2048 | tf_op jit(solution)/shard_map/psum | solution.py:101
  122.9 1.7 convolution_convert_fusion
  124.6 4.0 %copy.106 = bf16[48,64,256]{1,0,2:T(8,128)(2,1)S(1)} copy(bf16[48,64,256]{2,1,0:T(8,128)(2,1)} %convolution_convert_fusion) | data formatting | bytes 3145728 | tf_op jit(solution)/shard_map/reshape | solution.py:106
  128.7 5.5 %fusion.37 = f32[8,48,32,32]{1,3,2,0:T(8,128)} fusion(bf16[48,64,8,32]{1,0,3,2:T(8,128)(2,1)S(1)} %bitcast.94, bf16[32,64,8,1]{1,2,0,3:T(8,128)(2,1)S(1)} %fusion.39), kind=kOutput, calls=%fused_computation.52 | convolution fusion | flops 50331648 | bytes 3178496 | tf_op jit(solution)/shard_map/ijh,sjhc->sihc/dot_general | solution.py:109
  134.1 4.9 %copy.109 = f32[48,32,256]{2,1,0:T(8,128)} copy(f32[48,32,256]{0,1,2:T(8,128)} %bitcast.93) | data formatting | bytes 3145728 | tf_op jit(solution)/shard_map/reshape | solution.py:111
  139.1 47.1 %all-reduce.4.cloned.1.call-done = f32[48,32,256]{2,1,0:T(8,128)} async-done(((f32[48,32,256]{2,1,0:T(8,128)}), f32[48,32,256]{2,1,0:T(8,128)}) %all-reduce.4.cloned.1.call-update) | async-done | bytes 1572880 | tf_op jit(solution)/shard_map/psum | solution.py:110
  186.2 2.1 %fusion.19 = bf16[12,32,64]{2,1,0:T(8,128)(2,1)} fusion(f32[48,32,256]{2,1,0:T(8,128)} %all-reduce.4.cloned.1.call-done, s32[]{:T(128)S(6)} %select_n.8, bf16[12,32,64]{2,1,0:T(8,128)(2,1)S(1)} %copy-done.6, bf16[48,32,64]{2,1,0:T(8,128)(2,1)} %copy-done.3, bf16[256,64]{0,1:T(8,128)(2,1)S(1)} %copy-done.13, bf16[64,256]{1,0:T(8,128)(2,1)S(1)} %copy-done.14), kind=kOutput, calls=%fused_computation.29 | convolution fusion | flops 25731072 | bytes 656384 | tf_op jit(solution)/shard_map/dot_general | solution.py:125
  (60 shorter events, 1.0 us)
Async XLA Ops:
  7.2 115.8 %copy-start = (bf16[64,256]{1,0:T(8,128)(2,1)S(1)}, bf16[64,256]{1,0:T(8,128)(2,1)}, u32[]{:S(2)}) copy-start(bf16[64,256]{1,0:T(8,128)(2,1)} %param.23) | copy-start | bytes 98308
  32.5 11.5 %copy-start.6 = (bf16[12,32,64]{2,1,0:T(8,128)(2,1)S(1)}, bf16[12,32,64]{2,1,0:T(8,128)(2,1)}, u32[]{:S(2)}) copy-start(bf16[12,32,64]{2,1,0:T(8,128)(2,1)} %param.15) | copy-start | bytes 147460
  32.5 21.7 %copy-start.16 = (s32[12]{0:T(128)S(1)}, s32[12]{0:T(128)}, u32[]{:S(2)}) copy-start(s32[12]{0:T(128)} %param.17) | copy-start | bytes 148
  32.6 21.7 %copy-start.19 = (u32[32]{0:T(128)S(1)}, u32[32]{0:T(128)}, u32[]{:S(2)}) copy-start(u32[32]{0:T(128)} %constant.58) | copy-start | bytes 388
  33.9 28.3 %copy-start.18 = (u32[32]{0:T(128)S(1)}, u32[32]{0:T(128)}, u32[]{:S(2)}) copy-start(u32[32]{0:T(128)} %constant.53) | copy-start | bytes 388
  33.9 28.9 %copy-start.17 = (s32[32]{0:T(128)S(1)}, s32[32]{0:T(128)}, u32[]{:S(2)}) copy-start(s32[32]{0:T(128)} %param.16) | copy-start | bytes 388
  33.9 44.3 %copy-start.7 = (bf16[64,32]{0,1:T(8,128)(2,1)S(1)}, bf16[64,32]{0,1:T(8,128)(2,1)}, u32[]{:S(2)}) copy-start(bf16[64,32]{0,1:T(8,128)(2,1)} %param.18) | copy-start | bytes 12292
  33.9 44.9 %all-to-all-start = ((bf16[4,2,24576]{2,1,0:T(2,128)(2,1)}), bf16[4,2,24576]{2,1,0:T(2,128)(2,1)S(1)}, u32[]{:S(2)}, u32[]{:S(2)}) async-start(bf16[4,2,24576]{2,1,0:T(2,128)(2,1)} %reshape.169), calls=%async_computation | async-start | bytes 786432 | tf_op jit(solution)/shard_map/all_to_all | solution.py:52
  44.0 142.2 %all-reduce.4.cloned.1.call-start = ((), (), s32[]{:S(2)}) async-start(), calls=%async_computation.1 | async-start | bytes 3145728 | tf_op jit(solution)/shard_map/psum | solution.py:110
  62.2 16.6 %copy-start.3 = (bf16[48,32,64]{2,1,0:T(8,128)(2,1)}, bf16[48,32,64]{2,1,0:T(8,128)(2,1)S(1)}, u32[]{:S(2)}) copy-start(bf16[48,32,64]{2,1,0:T(8,128)(2,1)S(1)} %fusion.27) | copy-start | bytes 589828
  78.2 0.6 copy-start.9
  83.5 1.7 copy-start.8
  83.5 1.7 copy-start.10
  85.3 1.0 copy-start.1
  85.3 1.3 copy-start.4
  95.2 1.0 copy-start.5
  95.2 1.0 copy-start.11
  96.2 1.4 copy-start.12
  96.2 1.4 copy-start.15
  96.6 1.0 copy-start.2
  139.0 47.2 %copy-start.13 = (bf16[256,64]{0,1:T(8,128)(2,1)S(1)}, bf16[256,64]{0,1:T(8,128)(2,1)}, u32[]{:S(2)}) copy-start(bf16[256,64]{0,1:T(8,128)(2,1)} %param.25) | copy-start | bytes 98308
  139.0 47.2 %copy-start.14 = (bf16[64,256]{1,0:T(8,128)(2,1)S(1)}, bf16[64,256]{1,0:T(8,128)(2,1)}, u32[]{:S(2)}) copy-start(bf16[64,256]{1,0:T(8,128)(2,1)} %param.24) | copy-start | bytes 98308
Sparse Core Ops, SparseCore 0:
  139.2 46.9 all-reduce.3
where the time goes:
time: 197 us; the launch traced here: 195 us
  blocking collectives  77.4 us (39%)
  waiting for transfers between devices  47.1 us (24%)
  local copies, waits for them, and re-layouts  20.7 us (11%)
  matrix products  16.4 us (8%)
  between operations  15.8 us (8%)
  starting transfers between devices  10.1 us (5%)
  other arithmetic  7.48 us (4%)
    psum x1, waiting for transfers between devices, body(): lax.psum(summed.reshape(sequence_overall, homolog_flags, head_count * hea...  47.1 us
    all_gather x1, blocking collectives, body(): lax.all_gather(homolog_features, 'row', axis=1, tiled=True)  24.8 us
    unnamed x2, blocking collectives  18.2 us
    pmax x1, blocking collectives, body(): row_top = lax.pmax(jnp.max(logits, axis=1), 'col')  13.8 us
    psum x1, blocking collectives, body(): row_total = lax.psum(jnp.sum(expd, axis=1), 'col')  10.3 us
    all_gather x1, blocking collectives, body(): lax.all_gather(homolog_features, 'col', axis=0, tiled=True)  10.2 us
    all_to_all x1, starting transfers between devices, body(): lax.all_to_all(expanded_homologs, 'col', split_axis=1, concat_axis=0, til...  10.1 us
    dot_general x1, matrix products, body(): jnp.einsum('ijh,sjhc->sihc', weights, values_heads, preferred_element_typ...  5.46 us
  transfers between devices with their start and end apart: 2, of which 1 were waited for; matrix products, arithmetic and copies ran while one was open for 2% of the time, Pallas kernels for 0%

commit v1 on v0

v1 whole, which is shorter than its diff:
```python
import functools

import jax
import jax.numpy as jnp
from jax import lax
from jax.experimental import pallas as pl
from jax.experimental.pallas import tpu as pltpu
from jax.sharding import PartitionSpec as P

EPSILON = 1e-05
MESH = pl.DeviceIdType.MESH
BF16 = jnp.bfloat16
F32 = jnp.float32


def standardize(inputs):
    mean_value = jnp.mean(inputs, axis=-1, keepdims=True)
    centered = inputs - mean_value
    variance = jnp.mean(centered * centered, axis=-1, keepdims=True)
    return centered * lax.rsqrt(variance + EPSILON)


def kernel(
    R, C, S,
    couple, hom, norm, lblk, rblk, flags, w_dcz, offset, score, content, switch, final,
    pair_out, hom_out,
    lbuf, rbuf, nbuf, lgbuf, wbd, pbuf, ubuf, vbuf, gbuf, wtmp, mcol,
    lsend, lrecv, rsend, rrecv, nsend, nrecv, gsend, grecv,
):
    I, J, Z = couple.shape
    F = w_dcz.shape[0]
    H = score.shape[1]
    S2 = norm.shape[0]
    CH = norm.shape[2] // 2
    HC = content.shape[1]
    HV = J // I
    SP = lblk.shape[0]
    PK = Z // F
    IG = I // PK
    r = lax.axis_index("row")
    c = lax.axis_index("col")
    target = lax.div(r, HV)
    part = lax.rem(r, HV)
    own_target = target == c

    barrier = pltpu.get_barrier_semaphore()

    def greet(row, col):
        pl.semaphore_signal(barrier, inc=1, device_id=(row, col), device_id_type=MESH)

    for k in range(1, C):
        greet(r, lax.rem(c + k, C))
    for k in range(1, R):
        greet(lax.rem(r + k, R), c)
    for half in range(HV):
        for k in range(C):
            row, col = c * HV + half, lax.rem(c + k, C)
            if k == 0:
                pl.when(jnp.logical_not(row == r))(functools.partial(greet, row, col))
            else:
                greet(row, col)

    wbd[...] = jnp.zeros_like(wbd)
    for d in range(F):
        block = w_dcz[d]
        for p in range(PK):
            wbd[pl.ds(d * Z + p * F, F), pl.ds(p * Z, Z)] = block

    pl.semaphore_wait(barrier, (C - 1) + (R - 1) + R - own_target.astype(jnp.int32))

    def right_copy(k, row):
        return pltpu.make_async_remote_copy(
            src_ref=rblk, dst_ref=rbuf.at[part, c], send_sem=rsend.at[k],
            recv_sem=rrecv.at[part, c], device_id=(row, target), device_id_type=MESH)

    for k in range(1, R):
        right_copy(k, lax.rem(r + k, R)).start()

    @pl.when(jnp.logical_not(own_target))
    def _():
        right_copy(0, r).start()

    left_copies = []
    for k in range(1, C):
        copy = pltpu.make_async_remote_copy(
            src_ref=lblk, dst_ref=lbuf.at[c], send_sem=lsend.at[k],
            recv_sem=lrecv.at[c], device_id=(r, lax.rem(c + k, C)), device_id_type=MESH)
        copy.start()
        left_copies.append(copy)

    norm_copies = []
    for k in range(1, R):
        copy = pltpu.make_async_remote_copy(
            src_ref=norm, dst_ref=nbuf.at[r], send_sem=nsend.at[k],
            recv_sem=nrecv.at[r], device_id=(lax.rem(r + k, R), c), device_id_type=MESH)
        copy.start()
        norm_copies.append(copy)

    lbuf[c] = lblk[...]
    nbuf[r] = norm[...]

    @pl.when(own_target)
    def _():
        rbuf[part, c] = rblk[...]

    zero = jnp.zeros((CH, HC), BF16)

    def doubled(m):
        return jnp.concatenate(
            [jnp.concatenate([m, zero], axis=1), jnp.concatenate([zero, m], axis=1)], axis=0)

    switch2 = doubled(switch[...])
    for s in range(S2):
        gate = jnp.dot(norm[s], switch2, preferred_element_type=F32)
        gbuf[s] = 1.0 / (1.0 + jnp.exp(-gate))

    for k in range(1, C):
        peer = lax.rem(c + k, C)
        pltpu.make_async_remote_copy(
            src_ref=lblk, dst_ref=lbuf.at[peer], send_sem=lsend.at[k],
            recv_sem=lrecv.at[peer], device_id=(r, peer), device_id_type=MESH).wait_recv()
    for half in range(HV):
        for k in range(C):
            row, col = c * HV + half, lax.rem(c + k, C)

            def arrive(half=half, row=row, col=col, k=k):
                pltpu.make_async_remote_copy(
                    src_ref=rblk, dst_ref=rbuf.at[half, col], send_sem=rsend.at[k],
                    recv_sem=rrecv.at[half, col], device_id=(row, col),
                    device_id_type=MESH).wait_recv()

            if k == 0:
                pl.when(jnp.logical_not(row == r))(arrive)
            else:
                arrive()

    count = jnp.zeros((1, 1), F32)
    for k in range(C):
        count = count + lbuf[k][S + 1:S + 2, 0:1].astype(F32)
    inv = 1.0 / count
    left = lbuf[...].reshape(C * SP, I * F)
    step = Z // I
    for half in range(HV):
        def outer(t, carry, half=half):
            at = pl.multiple_of(t * Z, Z)
            lhs = rbuf[half, :, :, pl.ds(at, Z)].reshape(C * SP, Z)
            o = lax.dot_general(lhs, left, (((0,), (0,)), ((), ())),
                                preferred_element_type=F32).astype(BF16)
            for q in range(step):
                for g in range(IG):
                    pbuf[t, pl.ds(g * J + half * I, I), pl.ds(q * Z, Z)] = (
                        o[q * I:(q + 1) * I, g * Z:(g + 1) * Z])
            return carry
        lax.fori_loop(0, F // step, outer, 0)

    ubuf[...] = jnp.zeros_like(ubuf)

    def contract(t, carry):
        at = pl.multiple_of(t * (step * Z), step * Z)
        ubuf[...] += jnp.dot(pbuf[t], wbd[pl.ds(at, step * Z), :], preferred_element_type=F32)
        return carry
    lax.fori_loop(0, F // step, contract, 0)

    rows_of, lanes_of = (lax.broadcasted_iota(jnp.int32, (I, I), n) for n in (0, 1))
    lane_parts = []
    for half in range(HV):
        lane = rbuf[half, 0][S:S + 1, 0:I].astype(F32)
        lane_parts.append(lane)
        spread = jnp.where(rows_of == lanes_of, jnp.broadcast_to(lane, (I, I)), 0.0)
        mcol[pl.ds(half * I, I), :] = jnp.broadcast_to(
            jnp.sum(spread, axis=1, keepdims=True), (I, Z))
    bias = (jnp.concatenate(lane_parts * 2, axis=1) - 1.0) * 1000000000.0

    off = offset[...]
    score_t = score[...].astype(F32).T.astype(BF16)
    hi = I // 2
    own = lgbuf.at[c]

    def epilogue(g, carry):
        for p in range(PK):
            pieces = []
            for upper in range(2):
                i = g * PK + p + upper * hi
                row = pl.multiple_of((g + upper * (IG // 2)) * J, J)
                update = ubuf[pl.ds(row, J), p * Z:(p + 1) * Z] * inv + off
                mark = flags[i].astype(F32)
                new = (couple[i].astype(F32) + (mcol[...] * mark) * update).astype(BF16)
                pair_out[i] = new
                normed = standardize(new.astype(F32)).astype(BF16)
                pieces.append(lax.dot_general(
                    score_t, normed, (((1,), (1,)), ((), ())), preferred_element_type=F32))
            own[g * PK + p] = jnp.concatenate(pieces, axis=1) + bias
        return carry
    lax.fori_loop(0, IG // 2, epilogue, 0)

    logit_copies = []
    for k in range(1, C):
        copy = pltpu.make_async_remote_copy(
            src_ref=lgbuf.at[c], dst_ref=lgbuf.at[c], send_sem=gsend.at[k],
            recv_sem=grecv.at[c], device_id=(r, lax.rem(c + k, C)), device_id_type=MESH)
        copy.start()
        logit_copies.append(copy)

    for k in range(1, R):
        peer = lax.rem(r + k, R)
        pltpu.make_async_remote_copy(
            src_ref=norm, dst_ref=nbuf.at[peer], send_sem=nsend.at[k],
            recv_sem=nrecv.at[peer], device_id=(peer, c), device_id_type=MESH).wait_recv()
    content2 = doubled(content[...])

    def value(s, carry):
        x = nbuf[:, s].reshape(R * I, 2 * CH)
        vbuf[s] = jnp.dot(x, content2, preferred_element_type=F32).astype(BF16)
        return carry
    lax.fori_loop(0, S2, value, 0)

    for k in range(1, C):
        peer = lax.rem(c + k, C)
        pltpu.make_async_remote_copy(
            src_ref=lgbuf.at[peer], dst_ref=lgbuf.at[peer], send_sem=gsend.at[k],
            recv_sem=grecv.at[peer], device_id=(r, peer), device_id_type=MESH).wait_recv()

    for upper in range(2):
        logits = jnp.concatenate(
            [lgbuf[k].reshape(hi * H, 2 * J)[:, upper * J:(upper + 1) * J] for k in range(C)],
            axis=1)
        e = jnp.exp(logits - jnp.max(logits, axis=1, keepdims=True))
        wts = e / jnp.sum(e, axis=1, keepdims=True)
        for at in range(0, C * J, 128):
            wtmp[at // 128, pl.ds(upper * hi * H, hi * H), :] = wts[:, at:at + 128]
    weights = jnp.concatenate(
        [jnp.concatenate([wtmp[a, pl.ds(h, I, stride=H), :] for a in range(C * J // 128)], axis=1)
         for h in range(H)], axis=0).astype(BF16)

    head_lane = lax.rem(lax.broadcasted_iota(jnp.int32, (I, 2 * HC), 1), HC) // (HC // H)
    fin = final[...]

    for s in range(S2):
        full = jnp.dot(weights, vbuf[s], preferred_element_type=F32)
        acc = jnp.zeros((I, 2 * HC), F32)
        for h in range(H):
            acc = jnp.where(head_lane == h, full[h * I:(h + 1) * I], acc)
        gated = (gbuf[s] * acc).astype(BF16)
        for t in range(2):
            seq = s + t * S2
            if seq < S:
                res = jnp.dot(gated[:, t * HC:(t + 1) * HC], fin, preferred_element_type=F32)
                hom_out[seq] = (hom[seq].astype(F32) + res).astype(BF16)

    for k in range(1, R):
        right_copy(k, lax.rem(r + k, R)).wait_send()

    @pl.when(jnp.logical_not(own_target))
    def _():
        right_copy(0, r).wait_send()
    for copy in left_copies + norm_copies + logit_copies:
        copy.wait_send()


def solution(mesh):
    R, C = mesh.shape["row"], mesh.shape["col"]

    def body(couple, hom, flags, avail, w_left, w_right, w_con, offset, score, content, switch,
             final):
        S, I, CH = hom.shape
        J, Z = couple.shape[1:]
        F = w_left.shape[1]
        H = score.shape[1]
        HC = content.shape[1]
        S2 = (S + 1) // 2
        SP = -(-(S + 2) // 16) * 16
        norm = standardize(hom.astype(F32)).astype(BF16)
        marks = avail.astype(F32)
        left = (jnp.dot(norm, w_left, preferred_element_type=F32)
                * marks[:, None, None]).astype(BF16).reshape(S, I * F)
        right = (jnp.dot(norm, w_right, preferred_element_type=F32)
                 * marks[:, None, None]).astype(BF16).transpose(0, 2, 1).reshape(S, F * I)
        count = jnp.broadcast_to(jnp.sum(marks).astype(BF16), (1, I * F))
        pad = lambda n: jnp.zeros((n, I * F), BF16)
        lblk = jnp.concatenate([left, pad(1), count, pad(SP - S - 2)], axis=0)
        tok = jnp.tile(flags.astype(BF16), F)[None]
        rblk = jnp.concatenate([right, tok, pad(SP - S - 1)], axis=0)
        padded = jnp.pad(norm, ((0, 2 * S2 - S), (0, 0), (0, 0)))
        packed = jnp.concatenate([padded[:S2], padded[S2:]], axis=-1)
        w_dcz = w_con.reshape(F, F, Z).transpose(1, 0, 2)
        step = Z // I
        vmem = pl.BlockSpec(memory_space=pltpu.VMEM)
        smem = pl.BlockSpec(memory_space=pltpu.SMEM)
        dma = pltpu.SemaphoreType.DMA
        return pl.pallas_call(
            functools.partial(kernel, R, C, S),
            out_shape=(jax.ShapeDtypeStruct(couple.shape, BF16),
                       jax.ShapeDtypeStruct(hom.shape, BF16)),
            in_specs=[vmem] * 5 + [smem] + [vmem] * 6,
            out_specs=(vmem, vmem),
            scratch_shapes=[
                pltpu.VMEM((C, SP, I * F), BF16),
                pltpu.VMEM((J // I, C, SP, F * I), BF16),
                pltpu.VMEM((R, S2, I, 2 * CH), BF16),
                pltpu.VMEM((C, I // 2, H, 2 * J), F32),
                pltpu.VMEM((F * Z, Z // F * Z), BF16),
                pltpu.VMEM((F // step, I * F // Z * J, step * Z), BF16),
                pltpu.VMEM((I * F // Z * J, Z // F * Z), F32),
                pltpu.VMEM((S2, R * I, 2 * HC), BF16),
                pltpu.VMEM((S2, I, 2 * HC), F32),
                pltpu.VMEM((C * J // 128, I * H, 128), F32),
                pltpu.VMEM((J, Z), F32),
                dma((C,)), dma((C,)), dma((R,)), dma((J // I, C)),
                dma((R,)), dma((R,)), dma((C,)), dma((C,)),
            ],
            compiler_params=pltpu.CompilerParams(
                collective_id=0, has_side_effects=True, vmem_limit_bytes=56 * 2**20),
        )(couple, hom, packed, lblk, rblk, flags, w_dcz, offset.reshape(1, Z), score, content,
          switch, final)

    placed = (P("row", "col", None), P("col", "row", None), P("row"), P("col")) + (P(),) * 8
    return jax.shard_map(
        body, mesh=mesh, in_specs=placed,
        out_specs=(P("row", "col", None), P("col", "row", None)), check_vma=False)
```

time: 197 us -> 47.9 us (0.24)
  blocking collectives: 77.4 us -> 0 us
  waiting for transfers between devices: 47.1 us -> 0 us
  Pallas kernels: 0 us -> 33.8 us
  matrix products: 16.4 us -> 0.32 us
  between operations: 15.8 us -> 0.78 us
  local copies, waits for them, and re-layouts: 20.7 us -> 7.26 us
  starting transfers between devices: 10.1 us -> 0 us
  other arithmetic: 7.48 us -> 5.43 us
    psum x1 -> x0, waiting for transfers between devices: 47.1 us -> none  [body(): lax.psum(summed.reshape(sequence_overall, homolog_flags, head_count * hea...]
    all_gather x2 -> x0, blocking collectives: 35 us -> none  [the longest x1 24.8 us: body(): lax.all_gather(homolog_features, 'row', axis=1, tiled=True)]
    pallas_call x0 -> x1, Pallas kernels: none -> 33.8 us  [body(): pl.pallas_call(functools.partial(kernel, R, C, S), out_shape=(jax.ShapeDt...]
    unnamed x2 -> x0, blocking collectives: 18.2 us -> none
    dot_general x10 -> x2, matrix products: 16.4 us -> 0.32 us  [the longest x1 0.16 us: body(): jnp.dot(norm, w_left, preferred_element_type=F32) * marks[:, None, None]]
    pmax x1 -> x0, blocking collectives: 13.8 us -> none  [body(): row_top = lax.pmax(jnp.max(logits, axis=1), 'col')]
    psum x1 -> x0, blocking collectives: 10.3 us -> none  [body(): row_total = lax.psum(jnp.sum(expd, axis=1), 'col')]
    all_to_all x1 -> x0, starting transfers between devices: 10.1 us -> none  [body(): lax.all_to_all(expanded_homologs, 'col', split_axis=1, concat_axis=0, til...]
  transfers between devices with their start and end apart: 2 -> 0, of which waited for: 1 -> 0; matrix products, arithmetic and copies ran while one was open for 2% -> 0% of each run, Pallas kernels for 0% -> 0%
where the time goes in v1:
time: 47.9 us; the launch traced here: 47.6 us
  Pallas kernels  33.8 us (71%)
  local copies, waits for them, and re-layouts  7.26 us (15%)
  other arithmetic  5.43 us (11%)
  between operations  0.78 us (2%)
    pallas_call x1, Pallas kernels, body(): pl.pallas_call(functools.partial(kernel, R, C, S), out_shape=(jax.ShapeDt...  33.8 us
    unnamed x18, local copies, waits for them, and re-layouts  4.98 us
    reduce_sum x1, other arithmetic, body(): count = jnp.broadcast_to(jnp.sum(marks).astype(BF16), (1, I * F))  1.3 us
    reduce_sum x1, other arithmetic, standardize(): mean_value = jnp.mean(inputs, axis=-1, keepdims=True)  1.01 us

profile of v1, /device:TPU:13, one launch (start us, length us, event | category | flops | bytes accessed | tf_op | source)
XLA Modules:
  0.0 47.6 jit_solution(2753632367151624374)
XLA Ops:
  0.6 0.0 copy-start
  0.6 0.0 copy-start.1
  0.7 1.3 %convert_reduce_fusion.1 = bf16[]{:T(256)} fusion(s32[12]{0:T(128)} %param.15), kind=kLoop, calls=%fused_computation.19 | loop fusion | flops 23 | bytes 50 | tf_op jit(solution)/shard_map/reduce_sum | solution.py:278
  2.0 0.7 %pad.5.clone = bf16[16]{0:T(256)(128)(2,1)S(1)} pad(bf16[1]{0:T(256)(128)(2,1)} %bitcast.7, bf16[]{:T(256)} %constant.3), padding=13_2 | pad | bytes 36 | tf_op jit(solution)/shard_map/concatenate | solution.py:280
  2.7 0.7 %convert_element_type.27 = f32[12]{0:T(128)S(1)} convert(s32[12]{0:T(128)} %param.15) | non-fusion elementwise | flops 12 | bytes 96 | tf_op jit(solution)/shard_map/convert_element_type | solution.py:273
  3.3 0.7 %convert_element_type.32 = bf16[32]{0:T(256)(128)(2,1)S(1)} convert(s32[32]{0:T(128)} %flags.1) | non-fusion elementwise | flops 32 | bytes 192 | tf_op jit(solution)/shard_map/convert_element_type | solution.py:281
  4.0 0.1 pad.4.clone
  4.1 0.1 pad.2.clone
  4.1 0.1 pad.6.clone
  4.2 0.1 broadcast_in_dim_tile.3
  4.3 1.0 %convert_reduce_fusion = f32[12,32]{1,0:T(8,128)S(1)} fusion(bf16[12,32,64]{2,1,0:T(8,128)(2,1)} %hom.1), kind=kLoop, calls=%fused_computation.7 | loop fusion | flops 48768 | bytes 50688 | tf_op jit(solution)/shard_map/reduce_sum | solution.py:17
  5.4 0.0 copy-done.1
  5.4 0.0 copy-start.6
  5.4 0.2 fusion.5
  5.6 0.0 copy-start.4
  5.6 0.4 copy-done.6
  6.0 0.7 %copy.19.score = bf16[128,8]{1,0:T(8,128)(2,1)} copy(bf16[128,8]{0,1:T(8,128)(2,1)S(1)} %copy-done.6) | data formatting | bytes 4096 | tf_op args[8]
  6.8 0.0 copy-done.4
  6.8 0.7 %copy.20.final = bf16[256,64]{1,0:T(8,128)(2,1)} copy(bf16[256,64]{0,1:T(8,128)(2,1)S(1)} %copy-done.4) | data formatting | bytes 65536 | tf_op args[11]
  7.5 0.2 fusion.6
  7.7 0.0 copy-done
  7.7 0.2 fusion
  7.8 0.0 copy-start.5
  7.9 0.2 reshape.30
  8.0 0.5 %copy-done.5 = bf16[64,32]{0,1:T(8,128)(2,1)S(1)} copy-done((bf16[64,32]{0,1:T(8,128)(2,1)S(1)}, bf16[64,32]{0,1:T(8,128)(2,1)}, u32[]{:S(2)}) %copy-start.5) | copy-done | bytes 4120
  8.5 0.2 fusion.2
  8.7 0.1 copy.17
  8.8 0.2 reshape.31
  9.0 0.0 copy-start.2
  9.0 0.7 %maximum_maximum_fusion = (bf16[16,1024]{1,0:T(8,128)(2,1)}, bf16[16,1024]{1,0:T(8,128)(2,1)}) fusion(bf16[12,1024]{1,0:T(8,128)(2,1)S(1)} %reshape.30, bf16[16]{0:T(256)(128)(2,1)S(1)} %pad.6.clone, bf16[16]{0:T(256)(128)(2,1)S(1)} %pad.5.clone, bf16[16]{0:T(256)(128)(2,1)S(1)} %pad.4.clone, bf16[16]{0:T(256)(128)(2,1)S(1)} %pad.2.clone, ...), kind=kLoop, calls=%fused_computation.13 | loop fusion | flops 229376 | bytes 116864 | tf_op jit(solution)/shard_map/concatenate | solution.py:280
  9.7 0.7 %pad_maximum_fusion.norm = bf16[6,32,128]{2,1,0:T(8,128)(2,1)} fusion(bf16[6,32,64]{2,1,0:T(8,128)(2,1)S(1)} %get-tuple-element.3, bf16[6,32,64]{2,1,0:T(8,128)(2,1)S(1)} %get-tuple-element.2), kind=kLoop, calls=%fused_computation.12 | loop fusion | flops 98304 | bytes 98304 | tf_op jit(solution)/shard_map/concatenate | solution.py:284
  10.4 0.0 copy-done.2
  10.4 0.8 %copy.22 = bf16[32,32,128]{2,0,1:T(8,128)(2,1)} copy(bf16[32,32,128]{2,1,0:T(8,128)(2,1)S(1)} %bitcast.18) | data formatting | bytes 524288 | tf_op jit(solution)/shard_map/reshape | solution.py:285
  11.2 33.8 %shard_map.131 = (bf16[32,64,128]{2,1,0:T(8,128)(2,1)}, bf16[12,32,64]{2,1,0:T(8,128)(2,1)}) custom-call(bf16[32,64,128]{2,1,0:T(8,128)(2,1)} %couple.1, bf16[12,32,64]{2,1,0:T(8,128)(2,1)} %hom.1, bf16[6,32,128]{2,1,0:T(8,128)(2,1)} %pad_maximum_fusion.norm, bf16[16,1024]{1,0:T(8,128)(2,1)} %get-tuple-element.4.lblk, ...), custom_call_target="tpu_custom_call" | custom-call | tf_op jit(solution)/shard_map/pallas_call | solution.py:290
  45.0 0.0 copy-start.3
  45.1 1.9 %copy.25 = bf16[32,64,128]{2,1,0:T(8,128)(2,1)} copy(bf16[32,64,128]{2,1,0:T(8,128)(2,1)} %get-tuple-element.8) | data formatting | bytes 1048576
  47.0 0.0 copy-done.3
  47.0 0.6 %copy.26 = bf16[12,32,64]{2,1,0:T(8,128)(2,1)} copy(bf16[12,32,64]{2,1,0:T(8,128)(2,1)S(1)} %copy-done.3) | data formatting | bytes 98304
  (6 shorter events, 0.0 us)
Async XLA Ops:
  0.6 7.0 %copy-start = (bf16[64,32]{0,1:T(8,128)(2,1)S(1)}, bf16[64,32]{0,1:T(8,128)(2,1)}, u32[]{:S(2)}) copy-start(bf16[64,32]{0,1:T(8,128)(2,1)} %param.16) | copy-start | bytes 12292
  0.6 4.7 %copy-start.1 = (bf16[12,32,64]{2,1,0:T(8,128)(2,1)S(1)}, bf16[12,32,64]{2,1,0:T(8,128)(2,1)}, u32[]{:S(2)}) copy-start(bf16[12,32,64]{2,1,0:T(8,128)(2,1)} %hom.1) | copy-start | bytes 147460
  5.4 0.7 %copy-start.6 = (bf16[128,8]{0,1:T(8,128)(2,1)S(1)}, bf16[128,8]{0,1:T(8,128)(2,1)}, u32[]{:S(2)}) copy-start(bf16[128,8]{0,1:T(8,128)(2,1)} %param.20) | copy-start | bytes 6148
  5.6 1.2 %copy-start.4 = (bf16[256,64]{0,1:T(8,128)(2,1)S(1)}, bf16[256,64]{0,1:T(8,128)(2,1)}, u32[]{:S(2)}) copy-start(bf16[256,64]{0,1:T(8,128)(2,1)} %param.23) | copy-start | bytes 98308
  7.8 0.7 %copy-start.5 = (bf16[64,32]{0,1:T(8,128)(2,1)S(1)}, bf16[64,32]{0,1:T(8,128)(2,1)}, u32[]{:S(2)}) copy-start(bf16[64,32]{0,1:T(8,128)(2,1)} %param.17) | copy-start | bytes 12292
  9.0 1.4 %copy-start.2 = (bf16[1024,128]{1,0:T(8,128)(2,1)S(1)}, bf16[1024,128]{1,0:T(8,128)(2,1)}, u32[]{:S(2)}) copy-start(bf16[1024,128]{1,0:T(8,128)(2,1)} %param.18) | copy-start | bytes 786436
  45.0 1.9 %copy-start.3 = (bf16[12,32,64]{2,1,0:T(8,128)(2,1)S(1)}, bf16[12,32,64]{2,1,0:T(8,128)(2,1)}, u32[]{:S(2)}) copy-start(bf16[12,32,64]{2,1,0:T(8,128)(2,1)} %get-tuple-element.9) | copy-start | bytes 147460

commit v2 on v1

--- a/solution.py
+++ b/solution.py
@@ -22,14 +22,14 @@
 
 def kernel(
     R, C, S,
-    couple, hom, norm, lblk, rblk, flags, w_dcz, offset, score, content, switch, final,
-    pair_out, hom_out,
-    lbuf, rbuf, nbuf, lgbuf, wbd, pbuf, ubuf, vbuf, gbuf, wtmp, mcol,
+    couple, hom, flags, flag_row, avail, w_left, w_right, w_con, offset, score, content, switch,
+    final, pair_out, hom_out,
+    norm, lblk, rblk, wcon, gated, lbuf, rbuf, nbuf, lgbuf, wbd, pbuf, ubuf, vbuf, gbuf, wtmp, mcol,
     lsend, lrecv, rsend, rrecv, nsend, nrecv, gsend, grecv,
 ):
     I, J, Z = couple.shape
-    F = w_dcz.shape[0]
-    H = score.shape[1]
+    F = w_left.shape[0]
+    H = score.shape[0]
     S2 = norm.shape[0]
     CH = norm.shape[2] // 2
     HC = content.shape[1]
@@ -60,11 +60,41 @@
             else:
                 greet(row, col)
 
-    wbd[...] = jnp.zeros_like(wbd)
-    for d in range(F):
-        block = w_dcz[d]
-        for p in range(PK):
-            wbd[pl.ds(d * Z + p * F, F), pl.ds(p * Z, Z)] = block
+    normed = standardize(hom[...].reshape(S * I, CH).astype(F32)).astype(BF16)
+    if S % 2:
+        padded = jnp.concatenate([normed, jnp.zeros((I, CH), BF16)], axis=0)
+    else:
+        padded = normed
+    norm[...] = jnp.concatenate(
+        [padded[:S2 * I], padded[S2 * I:]], axis=1).reshape(S2, I, 2 * CH)
+    feat, lane = (lax.broadcasted_iota(jnp.int32, (F, I * F), n) for n in (0, 1))
+    low_f = (lax.rem(lane, F) == feat).astype(F32).astype(BF16)
+    high_f = (lax.div(lane, I) == feat).astype(F32).astype(BF16)
+    res, lane = (lax.broadcasted_iota(jnp.int32, (I, I * F), n) for n in (0, 1))
+    high_i = (lax.div(lane, F) == res).astype(F32)
+    low_i = (lax.rem(lane, I) == res).astype(F32)
+    seq, lane = (lax.broadcasted_iota(jnp.int32, (SP, S * I), n) for n in (0, 1))
+    mark = jnp.zeros((SP, S * I), F32)
+    count = jnp.int32(0)
+    for n in range(S):
+        mark = jnp.where(seq == n, avail[n].astype(F32), mark)
+        count = count + avail[n]
+    pick = jnp.where(lax.div(lane, I) == seq, mark, 0.0).astype(BF16)
+    rows = lax.broadcasted_iota(jnp.int32, (SP, I * F), 0)
+
+    def factors(weight, spread, keep):
+        wide = lax.dot_general(weight[...], spread, (((0,), (0,)), ((), ())),
+                               preferred_element_type=F32).astype(BF16)
+        every = jnp.dot(normed, wide, preferred_element_type=F32).reshape(S, I, I * F)
+        own = (every * keep[None]).astype(BF16).reshape(S * I, I * F)
+        return jnp.dot(pick, own, preferred_element_type=F32)
+
+    right = factors(w_right, high_f, low_i)
+    tok = jnp.dot(jnp.broadcast_to(flag_row[...].astype(F32), (SP, I)).astype(BF16),
+                  low_i.astype(BF16), preferred_element_type=F32)
+    rblk[...] = jnp.where(rows == S, tok, right).astype(BF16)
+    left = factors(w_left, low_f, high_i)
+    lblk[...] = jnp.where(rows == S + 1, count.astype(F32), left).astype(BF16)
 
     pl.semaphore_wait(barrier, (C - 1) + (R - 1) + R - own_target.astype(jnp.int32))
 
@@ -95,6 +125,13 @@
             recv_sem=nrecv.at[r], device_id=(lax.rem(r + k, R), c), device_id_type=MESH)
         copy.start()
         norm_copies.append(copy)
+
+    wcon[...] = w_con[...].astype(F32)
+    wbd[...] = jnp.zeros_like(wbd)
+    for d in range(F):
+        block = wcon[pl.ds(d, F, stride=F), :].astype(BF16)
+        for p in range(PK):
+            wbd[pl.ds(d * Z + p * F, F), pl.ds(p * Z, Z)] = block
 
     lbuf[c] = lblk[...]
     nbuf[r] = norm[...]
@@ -172,7 +209,7 @@
     bias = (jnp.concatenate(lane_parts * 2, axis=1) - 1.0) * 1000000000.0
 
     off = offset[...]
-    score_t = score[...].astype(F32).T.astype(BF16)
+    score_t = score[...]
     hi = I // 2
     own = lgbuf.at[c]
 
@@ -233,19 +270,19 @@
          for h in range(H)], axis=0).astype(BF16)
 
     head_lane = lax.rem(lax.broadcasted_iota(jnp.int32, (I, 2 * HC), 1), HC) // (HC // H)
-    fin = final[...]
 
     for s in range(S2):
         full = jnp.dot(weights, vbuf[s], preferred_element_type=F32)
         acc = jnp.zeros((I, 2 * HC), F32)
         for h in range(H):
             acc = jnp.where(head_lane == h, full[h * I:(h + 1) * I], acc)
-        gated = (gbuf[s] * acc).astype(BF16)
-        for t in range(2):
-            seq = s + t * S2
-            if seq < S:
-                res = jnp.dot(gated[:, t * HC:(t + 1) * HC], fin, preferred_element_type=F32)
-                hom_out[seq] = (hom[seq].astype(F32) + res).astype(BF16)
+        both = (gbuf[s] * acc).astype(BF16)
+        gated[s] = both[:, :HC]
+        gated[s + S2] = both[:, HC:]
+    moved = lax.dot_general(gated[...].reshape(2 * S2 * I, HC), final[...],
+                            (((1,), (1,)), ((), ())), preferred_element_type=F32)
+    hom_out[...] = (hom[...].astype(F32)
+                    + moved.reshape(2 * S2, I, CH)[:S]).astype(BF16)
 
     for k in range(1, R):
         right_copy(k, lax.rem(r + k, R)).wait_send()
@@ -269,20 +306,6 @@
         HC = content.shape[1]
         S2 = (S + 1) // 2
         SP = -(-(S + 2) // 16) * 16
-        norm = standardize(hom.astype(F32)).astype(BF16)
-        marks = avail.astype(F32)
-        left = (jnp.dot(norm, w_left, preferred_element_type=F32)
-                * marks[:, None, None]).astype(BF16).reshape(S, I * F)
-        right = (jnp.dot(norm, w_right, preferred_element_type=F32)
-                 * marks[:, None, None]).astype(BF16).transpose(0, 2, 1).reshape(S, F * I)
-        count = jnp.broadcast_to(jnp.sum(marks).astype(BF16), (1, I * F))
-        pad = lambda n: jnp.zeros((n, I * F), BF16)
-        lblk = jnp.concatenate([left, pad(1), count, pad(SP - S - 2)], axis=0)
-        tok = jnp.tile(flags.astype(BF16), F)[None]
-        rblk = jnp.concatenate([right, tok, pad(SP - S - 1)], axis=0)
-        padded = jnp.pad(norm, ((0, 2 * S2 - S), (0, 0), (0, 0)))
-        packed = jnp.concatenate([padded[:S2], padded[S2:]], axis=-1)
-        w_dcz = w_con.reshape(F, F, Z).transpose(1, 0, 2)
         step = Z // I
         vmem = pl.BlockSpec(memory_space=pltpu.VMEM)
         smem = pl.BlockSpec(memory_space=pltpu.SMEM)
@@ -291,9 +314,14 @@
             functools.partial(kernel, R, C, S),
             out_shape=(jax.ShapeDtypeStruct(couple.shape, BF16),
                        jax.ShapeDtypeStruct(hom.shape, BF16)),
-            in_specs=[vmem] * 5 + [smem] + [vmem] * 6,
+            in_specs=[vmem, vmem, smem, vmem, smem] + [vmem] * 8,
             out_specs=(vmem, vmem),
             scratch_shapes=[
+                pltpu.VMEM((S2, I, 2 * CH), BF16),
+                pltpu.VMEM((SP, I * F), BF16),
+                pltpu.VMEM((SP, F * I), BF16),
+                pltpu.VMEM((F * F, Z), F32),
+                pltpu.VMEM((2 * S2, I, HC), BF16),
                 pltpu.VMEM((C, SP, I * F), BF16),
                 pltpu.VMEM((J // I, C, SP, F * I), BF16),
                 pltpu.VMEM((R, S2, I, 2 * CH), BF16),
@@ -310,8 +338,8 @@
             ],
             compiler_params=pltpu.CompilerParams(
                 collective_id=0, has_side_effects=True, vmem_limit_bytes=56 * 2**20),
-        )(couple, hom, packed, lblk, rblk, flags, w_dcz, offset.reshape(1, Z), score, content,
-          switch, final)
+        )(couple, hom, flags, flags.reshape(1, I), avail, w_left.T, w_right.T, w_con,
+          offset.reshape(1, Z), score.T, content, switch, final.T)
 
     placed = (P("row", "col", None), P("col", "row", None), P("row"), P("col")) + (P(),) * 8
     return jax.shard_map(

time: 47.9 us -> 36.3 us (0.76)
  other arithmetic: 5.43 us -> 0 us
  local copies, waits for them, and re-layouts: 7.26 us -> 2.55 us
  Pallas kernels: 33.8 us -> 33 us
    reduce_sum x3 -> x0, other arithmetic: 2.54 us -> none  [the longest x1 1.3 us: body(): count = jnp.broadcast_to(jnp.sum(marks).astype(BF16), (1, I * F))]
    unnamed x18 -> x4, local copies, waits for them, and re-layouts: 4.98 us -> 2.55 us
    convert_element_type x3 -> x0, other arithmetic: 1.48 us -> none  [the longest x1 0.66 us: body(): tok = jnp.tile(flags.astype(BF16), F)[None]]
    concatenate x2 -> x0, other arithmetic: 1.4 us -> none  [the longest x1 0.7 us: body(): packed = jnp.concatenate([padded[:S2], padded[S2:]], axis=-1)]
    reshape x3 -> x0, local copies, waits for them, and re-layouts: 1.11 us -> none  [the longest x1 0.81 us: body(): w_dcz = w_con.reshape(F, F, Z).transpose(1, 0, 2)]
    concatenate x4 -> x0, local copies, waits for them, and re-layouts: 0.95 us -> none  [the longest x3 0.87 us: body(): lblk = jnp.concatenate([left, pad(1), count, pad(SP - S - 2)], axis=0)]
    pallas_call x1, Pallas kernels: 33.8 us -> 33 us  [body(): pl.pallas_call(functools.partial(kernel, R, C, S), out_shape=(jax.ShapeDt...]
where the time goes in v2:
time: 36.3 us; the launch traced here: 36.2 us
  Pallas kernels  33 us (91%)
  local copies, waits for them, and re-layouts  2.55 us (7%)
  between operations  0.65 us (2%)
    pallas_call x1, Pallas kernels, body(): pl.pallas_call(functools.partial(kernel, R, C, S), out_shape=(jax.ShapeDt...  33 us
    unnamed x4, local copies, waits for them, and re-layouts  2.55 us

profile of v2, /device:TPU:13, one launch (start us, length us, event | category | flops | bytes accessed | tf_op | source)
XLA Modules:
  0.0 36.2 jit_solution(3889796407511853548)
XLA Ops:
  0.6 33.0 %shard_map.131 = (bf16[32,64,128]{2,1,0:T(8,128)(2,1)}, bf16[12,32,64]{2,1,0:T(8,128)(2,1)}) custom-call(bf16[32,64,128]{2,1,0:T(8,128)(2,1)} %couple.1, bf16[12,32,64]{2,1,0:T(8,128)(2,1)} %hom.1, s32[32]{0:T(128)} %flags.1, s32[1,32]{1,0:T(1,128)} %bitcast.10, s32[12]{0:T(128)} %avail.1, bf16[32,64]{1,0:T(8,128)(2,1)} %bitcast.7, bf16[32,64]{1,0:T(8,128)(2,1)} %bitcast.8, ...), custom_call_target="tpu_custom_call" | custom-call | tf_op jit(solution)/shard_map/pallas_call | solution.py:313
  33.6 0.0 copy-start
  33.6 1.9 %copy.16 = bf16[32,64,128]{2,1,0:T(8,128)(2,1)} copy(bf16[32,64,128]{2,1,0:T(8,128)(2,1)} %get-tuple-element.4) | data formatting | bytes 1048576
  35.5 0.0 copy-done
  35.5 0.6 %copy.17 = bf16[12,32,64]{2,1,0:T(8,128)(2,1)} copy(bf16[12,32,64]{2,1,0:T(8,128)(2,1)S(1)} %copy-done) | data formatting | bytes 98304
Async XLA Ops:
  33.6 1.9 %copy-start = (bf16[12,32,64]{2,1,0:T(8,128)(2,1)S(1)}, bf16[12,32,64]{2,1,0:T(8,128)(2,1)}, u32[]{:S(2)}) copy-start(bf16[12,32,64]{2,1,0:T(8,128)(2,1)} %get-tuple-element.5) | copy-start | bytes 147460

commit v3 on v2

--- a/solution.py
+++ b/solution.py
@@ -118,14 +118,6 @@
         copy.start()
         left_copies.append(copy)
 
-    norm_copies = []
-    for k in range(1, R):
-        copy = pltpu.make_async_remote_copy(
-            src_ref=norm, dst_ref=nbuf.at[r], send_sem=nsend.at[k],
-            recv_sem=nrecv.at[r], device_id=(lax.rem(r + k, R), c), device_id_type=MESH)
-        copy.start()
-        norm_copies.append(copy)
-
     wcon[...] = w_con[...].astype(F32)
     wbd[...] = jnp.zeros_like(wbd)
     for d in range(F):
@@ -171,32 +163,42 @@
             else:
                 arrive()
 
+    norm_copies = []
+    for k in range(1, R):
+        copy = pltpu.make_async_remote_copy(
+            src_ref=norm, dst_ref=nbuf.at[r], send_sem=nsend.at[k],
+            recv_sem=nrecv.at[r], device_id=(lax.rem(r + k, R), c), device_id_type=MESH)
+        copy.start()
+        norm_copies.append(copy)
+
     count = jnp.zeros((1, 1), F32)
     for k in range(C):
         count = count + lbuf[k][S + 1:S + 2, 0:1].astype(F32)
     inv = 1.0 / count
     left = lbuf[...].reshape(C * SP, I * F)
-    step = Z // I
+    wide = min(256, F * I)
     for half in range(HV):
         def outer(t, carry, half=half):
-            at = pl.multiple_of(t * Z, Z)
-            lhs = rbuf[half, :, :, pl.ds(at, Z)].reshape(C * SP, Z)
+            at = pl.multiple_of(t * wide, wide)
+            lhs = rbuf[half, :, :, pl.ds(at, wide)].reshape(C * SP, wide)
             o = lax.dot_general(lhs, left, (((0,), (0,)), ((), ())),
                                 preferred_element_type=F32).astype(BF16)
-            for q in range(step):
+            for q in range(wide // I):
+                to = pl.multiple_of(t * (wide // I * Z) + q * Z, Z)
                 for g in range(IG):
-                    pbuf[t, pl.ds(g * J + half * I, I), pl.ds(q * Z, Z)] = (
+                    pbuf[pl.ds(g * J + half * I, I), pl.ds(to, Z)] = (
                         o[q * I:(q + 1) * I, g * Z:(g + 1) * Z])
             return carry
-        lax.fori_loop(0, F // step, outer, 0)
-
-    ubuf[...] = jnp.zeros_like(ubuf)
+        lax.fori_loop(0, F * I // wide, outer, 0)
+
+    tall = min(256, IG * J)
 
     def contract(t, carry):
-        at = pl.multiple_of(t * (step * Z), step * Z)
-        ubuf[...] += jnp.dot(pbuf[t], wbd[pl.ds(at, step * Z), :], preferred_element_type=F32)
+        at = pl.multiple_of(t * tall, tall)
+        ubuf[pl.ds(at, tall), :] = jnp.dot(
+            pbuf[pl.ds(at, tall), :], wbd[...], preferred_element_type=F32)
         return carry
-    lax.fori_loop(0, F // step, contract, 0)
+    lax.fori_loop(0, IG * J // tall, contract, 0)
 
     rows_of, lanes_of = (lax.broadcasted_iota(jnp.int32, (I, I), n) for n in (0, 1))
     lane_parts = []
@@ -212,6 +214,12 @@
     score_t = score[...]
     hi = I // 2
     own = lgbuf.at[c]
+
+    def logit_copy(slot, g, k):
+        piece = lgbuf.at[slot, pl.ds(g * PK, PK)]
+        return pltpu.make_async_remote_copy(
+            src_ref=piece, dst_ref=piece, send_sem=gsend.at[k, g],
+            recv_sem=grecv.at[slot, g], device_id=(r, lax.rem(c + k, C)), device_id_type=MESH)
 
     def epilogue(g, carry):
         for p in range(PK):
@@ -227,16 +235,10 @@
                 pieces.append(lax.dot_general(
                     score_t, normed, (((1,), (1,)), ((), ())), preferred_element_type=F32))
             own[g * PK + p] = jnp.concatenate(pieces, axis=1) + bias
+        for k in range(1, C):
+            logit_copy(c, g, k).start()
         return carry
     lax.fori_loop(0, IG // 2, epilogue, 0)
-
-    logit_copies = []
-    for k in range(1, C):
-        copy = pltpu.make_async_remote_copy(
-            src_ref=lgbuf.at[c], dst_ref=lgbuf.at[c], send_sem=gsend.at[k],
-            recv_sem=grecv.at[c], device_id=(r, lax.rem(c + k, C)), device_id_type=MESH)
-        copy.start()
-        logit_copies.append(copy)
 
     for k in range(1, R):
         peer = lax.rem(r + k, R)
@@ -252,10 +254,8 @@
     lax.fori_loop(0, S2, value, 0)
 
     for k in range(1, C):
-        peer = lax.rem(c + k, C)
-        pltpu.make_async_remote_copy(
-            src_ref=lgbuf.at[peer], dst_ref=lgbuf.at[peer], send_sem=gsend.at[k],
-            recv_sem=grecv.at[peer], device_id=(r, peer), device_id_type=MESH).wait_recv()
+        for g in range(IG // 2):
+            logit_copy(lax.rem(c + k, C), g, k).wait_recv()
 
     for upper in range(2):
         logits = jnp.concatenate(
@@ -290,8 +290,11 @@
     @pl.when(jnp.logical_not(own_target))
     def _():
         right_copy(0, r).wait_send()
-    for copy in left_copies + norm_copies + logit_copies:
+    for copy in left_copies + norm_copies:
         copy.wait_send()
+    for k in range(1, C):
+        for g in range(IG // 2):
+            logit_copy(c, g, k).wait_send()
 
 
 def solution(mesh):
@@ -306,7 +309,6 @@
         HC = content.shape[1]
         S2 = (S + 1) // 2
         SP = -(-(S + 2) // 16) * 16
-        step = Z // I
         vmem = pl.BlockSpec(memory_space=pltpu.VMEM)
         smem = pl.BlockSpec(memory_space=pltpu.SMEM)
         dma = pltpu.SemaphoreType.DMA
@@ -327,14 +329,14 @@
                 pltpu.VMEM((R, S2, I, 2 * CH), BF16),
                 pltpu.VMEM((C, I // 2, H, 2 * J), F32),
                 pltpu.VMEM((F * Z, Z // F * Z), BF16),
-                pltpu.VMEM((F // step, I * F // Z * J, step * Z), BF16),
+                pltpu.VMEM((I * F // Z * J, F * Z), BF16),
                 pltpu.VMEM((I * F // Z * J, Z // F * Z), F32),
                 pltpu.VMEM((S2, R * I, 2 * HC), BF16),
                 pltpu.VMEM((S2, I, 2 * HC), F32),
                 pltpu.VMEM((C * J // 128, I * H, 128), F32),
                 pltpu.VMEM((J, Z), F32),
                 dma((C,)), dma((C,)), dma((R,)), dma((J // I, C)),
-                dma((R,)), dma((R,)), dma((C,)), dma((C,)),
+                dma((R,)), dma((R,)), dma((C, I * F // Z // 2)), dma((C, I * F // Z // 2)),
             ],
             compiler_params=pltpu.CompilerParams(
                 collective_id=0, has_side_effects=True, vmem_limit_bytes=56 * 2**20),

time: 36.3 us -> 31.3 us (0.86)
  Pallas kernels: 33 us -> 27.9 us
    pallas_call x1, Pallas kernels: 33 us -> 27.9 us  [body(): pl.pallas_call(functools.partial(kernel, R, C, S), out_shape=(jax.ShapeDt...]
where the time goes in v3:
time: 31.3 us; the launch traced here: 31.1 us
  Pallas kernels  27.9 us (89%)
  local copies, waits for them, and re-layouts  2.55 us (8%)
  between operations  0.65 us (2%)
    pallas_call x1, Pallas kernels, body(): pl.pallas_call(functools.partial(kernel, R, C, S), out_shape=(jax.ShapeDt...  27.9 us
    unnamed x4, local copies, waits for them, and re-layouts  2.55 us

profile of v3, /device:TPU:13, one launch (start us, length us, event | category | flops | bytes accessed | tf_op | source)
XLA Modules:
  0.0 31.1 jit_solution(12980356829374472713)
XLA Ops:
  0.6 27.9 %shard_map.131 = (bf16[32,64,128]{2,1,0:T(8,128)(2,1)}, bf16[12,32,64]{2,1,0:T(8,128)(2,1)}) custom-call(bf16[32,64,128]{2,1,0:T(8,128)(2,1)} %couple.1, bf16[12,32,64]{2,1,0:T(8,128)(2,1)} %hom.1, s32[32]{0:T(128)} %flags.1, s32[1,32]{1,0:T(1,128)} %bitcast.10, s32[12]{0:T(128)} %avail.1, bf16[32,64]{1,0:T(8,128)(2,1)} %bitcast.7, bf16[32,64]{1,0:T(8,128)(2,1)} %bitcast.8, ...), custom_call_target="tpu_custom_call" | custom-call | tf_op jit(solution)/shard_map/pallas_call | solution.py:315
  28.6 0.0 copy-start
  28.6 1.9 %copy.16 = bf16[32,64,128]{2,1,0:T(8,128)(2,1)} copy(bf16[32,64,128]{2,1,0:T(8,128)(2,1)} %get-tuple-element.4) | data formatting | bytes 1048576
  30.5 0.0 copy-done
  30.5 0.6 %copy.17 = bf16[12,32,64]{2,1,0:T(8,128)(2,1)} copy(bf16[12,32,64]{2,1,0:T(8,128)(2,1)S(1)} %copy-done) | data formatting | bytes 98304
Async XLA Ops:
  28.6 1.9 %copy-start = (bf16[12,32,64]{2,1,0:T(8,128)(2,1)S(1)}, bf16[12,32,64]{2,1,0:T(8,128)(2,1)}, u32[]{:S(2)}) copy-start(bf16[12,32,64]{2,1,0:T(8,128)(2,1)} %get-tuple-element.5) | copy-start | bytes 147460

commit v4 on v3

--- a/solution.py
+++ b/solution.py
@@ -314,8 +314,7 @@
         dma = pltpu.SemaphoreType.DMA
         return pl.pallas_call(
             functools.partial(kernel, R, C, S),
-            out_shape=(jax.ShapeDtypeStruct(couple.shape, BF16),
-                       jax.ShapeDtypeStruct(hom.shape, BF16)),
+            out_shape=(pltpu.VMEM(couple.shape, BF16), pltpu.VMEM(hom.shape, BF16)),
             in_specs=[vmem, vmem, smem, vmem, smem] + [vmem] * 8,
             out_specs=(vmem, vmem),
             scratch_shapes=[

time: 31.3 us -> 29.3 us (0.936)
  local copies, waits for them, and re-layouts: 2.55 us -> 1.44 us
  Pallas kernels: 27.9 us -> 27.1 us
    unnamed x4 -> x2, local copies, waits for them, and re-layouts: 2.55 us -> 1.44 us
    pallas_call x1, Pallas kernels: 27.9 us -> 27.1 us  [body(): pl.pallas_call(functools.partial(kernel, R, C, S), out_shape=(pltpu.VMEM(...]
where the time goes in v4:
time: 29.3 us; the launch traced here: 29.2 us
  Pallas kernels  27.1 us (92%)
  local copies, waits for them, and re-layouts  1.44 us (5%)
  between operations  0.64 us (2%)
    pallas_call x1, Pallas kernels, body(): pl.pallas_call(functools.partial(kernel, R, C, S), out_shape=(pltpu.VMEM(...  27.1 us
    unnamed x2, local copies, waits for them, and re-layouts  1.44 us

profile of v4, /device:TPU:13, one launch (start us, length us, event | category | flops | bytes accessed | tf_op | source)
XLA Modules:
  0.0 29.2 jit_solution(8527090520661260231)
XLA Ops:
  0.6 27.1 %shard_map.131 = (bf16[32,64,128]{2,1,0:T(8,128)(2,1)S(1)}, bf16[12,32,64]{2,1,0:T(8,128)(2,1)S(1)}) custom-call(bf16[32,64,128]{2,1,0:T(8,128)(2,1)} %couple.1, bf16[12,32,64]{2,1,0:T(8,128)(2,1)} %hom.1, s32[32]{0:T(128)} %flags.1, s32[1,32]{1,0:T(1,128)} %bitcast.10, s32[12]{0:T(128)} %avail.1, bf16[32,64]{1,0:T(8,128)(2,1)} %bitcast.7, ...), custom_call_target="tpu_custom_call" | custom-call | tf_op jit(solution)/shard_map/pallas_call | solution.py:315
  27.7 0.8 %copy.16 = bf16[32,64,128]{2,1,0:T(8,128)(2,1)} copy(bf16[32,64,128]{2,1,0:T(8,128)(2,1)S(1)} %get-tuple-element.2) | data formatting | bytes 1048576
  28.5 0.6 %copy.17 = bf16[12,32,64]{2,1,0:T(8,128)(2,1)} copy(bf16[12,32,64]{2,1,0:T(8,128)(2,1)S(1)} %get-tuple-element.3) | data formatting | bytes 98304
